TPU v7x, 32 devices: a whole 2x2x4 slice. The times are simulated.
32 devices in a mesh: dp: 16 (over z, y, core), mp: 2 (over x).
Axes of the slice: x: 2, y: 2, z: 4, core: 2. Of those that a mesh axis runs over, the one named last changes fastest.
Arguments:
- tokens: bfloat16 [24576, 768], P('dp'), may hold values from -6 to 6
- out_grad: bfloat16 [24576, 768], P('dp'), may hold values from -6 to 6
- doc_lengths: int32 [16, 4], P('dp'), may hold values from 1 to 1024, 1536 in all within a row
- w_query: float32 [768, 768], P('dp', 'mp'), may hold values from -0.21875 to 0.21875
- w_key: float32 [768, 768], P('dp', 'mp'), may hold values from -0.21875 to 0.21875
- w_value: float32 [768, 768], P('dp', 'mp'), may hold values from -0.21875 to 0.21875
- w_out: float32 [768, 768], P('mp', 'dp'), may hold values from -0.875 to 0.875
- gain_one: float32 [768], P('dp'), may hold values from 0.5 to 1.5
- w_gate: float32 [768, 2560], P('dp', 'mp'), may hold values from -0.21875 to 0.21875
- w_up: float32 [768, 2560], P('dp', 'mp'), may hold values from -0.21875 to 0.21875
- w_down: float32 [2560, 768], P('mp', 'dp'), may hold values from -0.125 to 0.125
- gain_two: float32 [768], P('dp'), may hold values from 0.5 to 1.5
Outputs:
- output: bfloat16 [24576, 768], P('dp')
- grad_tokens: float32 [24576, 768], P('dp')
- grad_w_query: float32 [768, 768], P('dp', 'mp')
- grad_w_key: float32 [768, 768], P('dp', 'mp')
- grad_w_value: float32 [768, 768], P('dp', 'mp')
- grad_w_out: float32 [768, 768], P('mp', 'dp')
- grad_gain_one: float32 [768], P('dp')
- grad_w_gate: float32 [768, 2560], P('dp', 'mp')
- grad_w_up: float32 [768, 2560], P('dp', 'mp')
- grad_w_down: float32 [2560, 768], P('mp', 'dp')
- grad_gain_two: float32 [768], P('dp')
Inputs may be any that keep to these rules, and one draw needn't show every extreme that they name: `doc_lengths`: each row lists the lengths of the 4 documents packed into one pack of 1536 tokens, in order; they sum to 1536 and the largest is exactly 1024.
All inputs are finite; a program needn't handle non-finite values.
Results may differ from a plain program's by a relative error of at most 0.019.
The roundings to bfloat16 on the way count: a program that leaves them out, or rounds other values in their place, can miss the bound.
Values may be sent and summed in bfloat16 or wider, within the bound.
A program may use at most 256 MiB of HBM per device.

v0:
```python
import math

import jax
import jax.numpy as jnp
from jax import lax
from jax.sharding import PartitionSpec as P

HD = 48
BLOCK = 512


NORM_EPS = 1e-05
NEG_FILL = -1000000000.0


def rope_tables(positions):
    half_dim = HD // 2
    frequency = jnp.exp(jnp.arange(half_dim, dtype=jnp.float32) * (-2.0 * math.log(10000.0) / HD))
    angles = positions.astype(jnp.float32)[:, None] * frequency[None, :]
    cos_table = jnp.cos(angles)
    sine_table = jnp.sin(angles)
    return (
        jnp.concatenate([cos_table, cos_table], 1),
        jnp.concatenate([sine_table, sine_table], 1),
    )


def rotate_half(head_vals):
    half_dim = head_vals.shape[-1] // 2
    return jnp.concatenate([-head_vals[..., half_dim:], head_vals[..., :half_dim]], -1)


def apply_rope(head_vals, cos_table, sine_table):
    return head_vals * cos_table[:, None, :] + rotate_half(head_vals) * sine_table[:, None, :]


def rope_back(head_grads, cos_table, sine_table):
    half_dim = head_grads.shape[-1] // 2
    turned = head_grads * sine_table[:, None, :]
    return head_grads * cos_table[:, None, :] + jnp.concatenate(
        [turned[..., half_dim:], -turned[..., :half_dim]], -1
    )


def doc_layout(lengths, token_count):
    doc_ends = jnp.cumsum(lengths, dtype=jnp.int32)
    starts = doc_ends - lengths
    token_index = jnp.arange(token_count, dtype=jnp.int32)
    doc_ids = jnp.sum(
        (token_index[:, None] >= doc_ends[None, :]).astype(jnp.int32), 1, dtype=jnp.int32
    )
    doc_picks = doc_ids[:, None] == jnp.arange(lengths.shape[0], dtype=jnp.int32)[None, :]
    start_of = jnp.sum(jnp.where(doc_picks, starts[None, :], 0), 1, dtype=jnp.int32)
    return (doc_ids, token_index - start_of)


def rms_forward(resid):
    inverse = lax.rsqrt(jnp.mean(resid * resid, -1, keepdims=True) + NORM_EPS)
    return (resid * inverse, inverse)


def rms_backward(grad_normed, normed, inverse):
    return inverse * (grad_normed - normed * jnp.mean(grad_normed * normed, -1, keepdims=True))


def masked_scores(query_block, key_rot, doc_block, index_block, doc_ids, token_index):
    raw_scores = jnp.einsum(
        "qhd,khd->hqk", query_block, key_rot, preferred_element_type=jnp.float32
    ) * HD ** (-0.5)
    allowed = (doc_block[:, None] == doc_ids[None, :]) & (
        index_block[:, None] >= token_index[None, :]
    )
    return jnp.where(allowed[None], raw_scores, NEG_FILL)


def on_device(
    tokens,
    out_grad,
    doc_lengths,
    w_query,
    w_key,
    w_value,
    w_out,
    gain_one,
    w_gate,
    w_up,
    w_down,
    gain_two,
):
    query_full, key_full, value_full, out_full, gain_a = (
        lax.all_gather(w_query.astype(jnp.bfloat16), "dp", axis=0, tiled=True),
        lax.all_gather(w_key.astype(jnp.bfloat16), "dp", axis=0, tiled=True),
        lax.all_gather(w_value.astype(jnp.bfloat16), "dp", axis=0, tiled=True),
        lax.all_gather(w_out.astype(jnp.bfloat16), "dp", axis=1, tiled=True),
        lax.all_gather(gain_one.astype(jnp.bfloat16), "dp", axis=0, tiled=True),
    )
    gate_full, up_full, down_full, gain_b = (
        lax.all_gather(w_gate.astype(jnp.bfloat16), "dp", axis=0, tiled=True),
        lax.all_gather(w_up.astype(jnp.bfloat16), "dp", axis=0, tiled=True),
        lax.all_gather(w_down.astype(jnp.bfloat16), "dp", axis=1, tiled=True),
        lax.all_gather(gain_two.astype(jnp.bfloat16), "dp", axis=0, tiled=True),
    )
    token_count = tokens.shape[0]
    heads_local = query_full.shape[1] // HD
    head_shape = (token_count, heads_local, HD)
    blocks = token_count // BLOCK
    score_scale = HD ** (-0.5)
    doc_ids, positions = doc_layout(doc_lengths[0], token_count)
    cos_table, sine_table = rope_tables(positions)
    token_index = jnp.arange(token_count, dtype=jnp.int32)
    doc_split = doc_ids.reshape(blocks, BLOCK)
    index_split = token_index.reshape(blocks, BLOCK)
    query_rot = apply_rope(
        jnp.dot(tokens, query_full, preferred_element_type=jnp.float32).reshape(head_shape),
        cos_table,
        sine_table,
    ).astype(jnp.bfloat16)
    key_rot = apply_rope(
        jnp.dot(tokens, key_full, preferred_element_type=jnp.float32).reshape(head_shape),
        cos_table,
        sine_table,
    ).astype(jnp.bfloat16)
    value_heads = (
        jnp.dot(tokens, value_full, preferred_element_type=jnp.float32)
        .astype(jnp.bfloat16)
        .reshape(head_shape)
    )
    query_blocks = query_rot.reshape(blocks, BLOCK, heads_local, HD)

    def forward_block(pieces):
        query_block, doc_block, index_block = pieces
        masked = masked_scores(query_block, key_rot, doc_block, index_block, doc_ids, token_index)
        row_top = jnp.max(masked, -1, keepdims=True)
        weights = jnp.exp(masked - row_top)
        row_totals = jnp.sum(weights, -1, keepdims=True)
        soft_probs = (weights / row_totals).astype(jnp.bfloat16)
        mixed_block = jnp.einsum(
            "hqk,khd->qhd", soft_probs, value_heads, preferred_element_type=jnp.float32
        )
        return (mixed_block, (row_top + jnp.log(row_totals))[..., 0])

    mixed_blocks, log_totals = lax.map(forward_block, (query_blocks, doc_split, index_split))
    mixed_flat = mixed_blocks.reshape(token_count, heads_local * HD).astype(jnp.bfloat16)
    attn_part = jnp.dot(mixed_flat, out_full, preferred_element_type=jnp.float32).astype(
        jnp.bfloat16
    )
    attn_total = lax.psum(attn_part, "mp").astype(jnp.float32)
    resid_one = tokens.astype(jnp.float32) + attn_total
    normed_one, inverse_one = rms_forward(resid_one)
    gain_one_f = gain_a.astype(jnp.float32)
    hidden = normed_one * gain_one_f
    hidden_bf = hidden.astype(jnp.bfloat16)
    gate_proj = jnp.dot(hidden_bf, gate_full, preferred_element_type=jnp.float32)
    up_proj = jnp.dot(hidden_bf, up_full, preferred_element_type=jnp.float32)
    sigmoid_gate = jax.nn.sigmoid(gate_proj)
    activated = (gate_proj * sigmoid_gate * up_proj).astype(jnp.bfloat16)
    ffn_part = jnp.dot(activated, down_full, preferred_element_type=jnp.float32).astype(
        jnp.bfloat16
    )
    ffn_total = lax.psum(ffn_part, "mp").astype(jnp.float32)
    resid_two = hidden + ffn_total
    normed_two, inverse_two = rms_forward(resid_two)
    gain_two_f = gain_b.astype(jnp.float32)
    output = (normed_two * gain_two_f).astype(jnp.bfloat16)
    grad_out = out_grad.astype(jnp.float32)
    grad_gain_two = jnp.sum(grad_out * normed_two, 0)
    grad_resid_two = rms_backward(grad_out * gain_two_f, normed_two, inverse_two)
    grad_ffn = grad_resid_two.astype(jnp.bfloat16)
    grad_down = jnp.einsum("tf,td->fd", activated, grad_ffn, preferred_element_type=jnp.float32)
    grad_act = jnp.einsum("td,fd->tf", grad_ffn, down_full, preferred_element_type=jnp.float32)
    grad_up_proj = (grad_act * gate_proj * sigmoid_gate).astype(jnp.bfloat16)
    grad_gate_proj = (
        grad_act * up_proj * sigmoid_gate * (1.0 + gate_proj * (1.0 - sigmoid_gate))
    ).astype(jnp.bfloat16)
    grad_gate = jnp.einsum(
        "td,tf->df", hidden_bf, grad_gate_proj, preferred_element_type=jnp.float32
    )
    grad_up = jnp.einsum("td,tf->df", hidden_bf, grad_up_proj, preferred_element_type=jnp.float32)
    hidden_term = jnp.einsum(
        "tf,df->td", grad_gate_proj, gate_full, preferred_element_type=jnp.float32
    ) + jnp.einsum("tf,df->td", grad_up_proj, up_full, preferred_element_type=jnp.float32)
    grad_hidden = grad_resid_two + lax.psum(hidden_term.astype(jnp.bfloat16), "mp").astype(
        jnp.float32
    )
    grad_gain_one = jnp.sum(grad_hidden * normed_one, 0)
    grad_resid_one = rms_backward(grad_hidden * gain_one_f, normed_one, inverse_one)
    grad_attn = grad_resid_one.astype(jnp.bfloat16)
    grad_out_proj = jnp.einsum(
        "th,td->hd", mixed_flat, grad_attn, preferred_element_type=jnp.float32
    )
    grad_mixed = (
        jnp.einsum("td,hd->th", grad_attn, out_full, preferred_element_type=jnp.float32)
        .astype(jnp.bfloat16)
        .reshape(blocks, BLOCK, heads_local, HD)
    )

    def backward_block(carry, pieces):
        grad_keys, grad_values = carry
        query_block, grad_block, log_block, doc_block, index_block = pieces
        masked = masked_scores(query_block, key_rot, doc_block, index_block, doc_ids, token_index)
        soft_probs = jnp.exp(masked - log_block[..., None])
        grad_probs = jnp.einsum(
            "qhd,khd->hqk", grad_block, value_heads, preferred_element_type=jnp.float32
        )
        row_dot = jnp.sum(soft_probs * grad_probs, -1, keepdims=True)
        grad_scores = (soft_probs * (grad_probs - row_dot)).astype(jnp.bfloat16)
        grad_query = (
            jnp.einsum("hqk,khd->qhd", grad_scores, key_rot, preferred_element_type=jnp.float32)
            * score_scale
        )
        grad_keys = (
            grad_keys
            + jnp.einsum(
                "hqk,qhd->khd", grad_scores, query_block, preferred_element_type=jnp.float32
            )
            * score_scale
        )
        grad_values = grad_values + jnp.einsum(
            "hqk,qhd->khd",
            soft_probs.astype(jnp.bfloat16),
            grad_block,
            preferred_element_type=jnp.float32,
        )
        return ((grad_keys, grad_values), grad_query)

    empty_heads = jnp.zeros(head_shape, jnp.float32)
    (grad_keys, grad_values), grad_queries = lax.scan(
        backward_block,
        (empty_heads, empty_heads),
        (query_blocks, grad_mixed, log_totals, doc_split, index_split),
    )
    flat_shape = (token_count, heads_local * HD)
    grad_query_raw = (
        rope_back(grad_queries.reshape(head_shape), cos_table, sine_table)
        .reshape(flat_shape)
        .astype(jnp.bfloat16)
    )
    grad_key_raw = (
        rope_back(grad_keys, cos_table, sine_table).reshape(flat_shape).astype(jnp.bfloat16)
    )
    grad_value_raw = grad_values.reshape(flat_shape).astype(jnp.bfloat16)
    grad_wq = jnp.einsum("td,th->dh", tokens, grad_query_raw, preferred_element_type=jnp.float32)
    grad_wk = jnp.einsum("td,th->dh", tokens, grad_key_raw, preferred_element_type=jnp.float32)
    grad_wv = jnp.einsum("td,th->dh", tokens, grad_value_raw, preferred_element_type=jnp.float32)
    token_term = jnp.einsum(
        "th,dh->td", grad_query_raw, query_full, preferred_element_type=jnp.float32
    )
    token_term = token_term + jnp.einsum(
        "th,dh->td", grad_key_raw, key_full, preferred_element_type=jnp.float32
    )
    token_term = token_term + jnp.einsum(
        "th,dh->td", grad_value_raw, value_full, preferred_element_type=jnp.float32
    )
    grad_tokens = grad_resid_one + lax.psum(token_term.astype(jnp.bfloat16), "mp").astype(
        jnp.float32
    )
    summed = (
        lax.psum_scatter(grad_wq, "dp", scatter_dimension=0, tiled=True),
        lax.psum_scatter(grad_wk, "dp", scatter_dimension=0, tiled=True),
        lax.psum_scatter(grad_wv, "dp", scatter_dimension=0, tiled=True),
        lax.psum_scatter(grad_out_proj, "dp", scatter_dimension=1, tiled=True),
        lax.psum_scatter(grad_gain_one, "dp", scatter_dimension=0, tiled=True),
        lax.psum_scatter(grad_gate, "dp", scatter_dimension=0, tiled=True),
        lax.psum_scatter(grad_up, "dp", scatter_dimension=0, tiled=True),
        lax.psum_scatter(grad_down, "dp", scatter_dimension=1, tiled=True),
        lax.psum_scatter(grad_gain_two, "dp", scatter_dimension=0, tiled=True),
    )
    return (
        output,
        grad_tokens,
        summed[0],
        summed[1],
        summed[2],
        summed[3],
        summed[4],
        summed[5],
        summed[6],
        summed[7],
        summed[8],
    )


def solution(mesh):
    placed = (
        P("dp", None),
        P("dp", None),
        P("dp", None),
        P("dp", "mp"),
        P("dp", "mp"),
        P("dp", "mp"),
        P("mp", "dp"),
        P("dp"),
        P("dp", "mp"),
        P("dp", "mp"),
        P("mp", "dp"),
        P("dp"),
    )
    return jax.shard_map(
        on_device,
        mesh=mesh,
        in_specs=placed,
        out_specs=(
            P("dp", None),
            P("dp", None),
            P("dp", "mp"),
            P("dp", "mp"),
            P("dp", "mp"),
            P("mp", "dp"),
            P("dp"),
            P("dp", "mp"),
            P("dp", "mp"),
            P("mp", "dp"),
            P("dp"),
        ),
        check_vma=False,
    )
```

profile of v0, /device:TPU:1, one launch (start us, length us, event | category | flops | bytes accessed | tf_op | source)
XLA Modules:
  0.0 1397.2 jit_solution(2624690552880834379)
XLA Ops:
  18.4 26.1 %all_gather.30 = bf16[384,768]{0,1:T(8,128)(2,1)} all-gather(bf16[384,48]{0,1:T(8,128)(2,1)S(1)} %convert_element_type.152), channel_id=1, replica_groups=mesh['dp'=16,'mp'=2] {'dp'}, dimensions={1}, use_global_device_ids=true | all-gather | bytes 626688 | tf_op jit(solution)/shard_map/all_gather | solution.py:94
  44.5 19.0 %all_gather.29 = bf16[768,384]{1,0:T(8,128)(2,1)S(1)} all-gather(bf16[48,384]{1,0:T(8,128)(2,1)S(1)} %convert_element_type.148), channel_id=1, replica_groups=mesh['dp'=16,'mp'=2] {'dp'}, dimensions={0}, use_global_device_ids=true | all-gather | bytes 626688 | tf_op jit(solution)/shard_map/all_gather | solution.py:93
  63.5 20.4 %all_gather.28 = bf16[768,384]{1,0:T(8,128)(2,1)S(1)} all-gather(bf16[48,384]{1,0:T(8,128)(2,1)S(1)} %convert_element_type.145), channel_id=1, replica_groups=mesh['dp'=16,'mp'=2] {'dp'}, dimensions={0}, use_global_device_ids=true | all-gather | bytes 626688 | tf_op jit(solution)/shard_map/all_gather | solution.py:92
  84.0 19.0 %all_gather.27 = bf16[768,384]{1,0:T(8,128)(2,1)S(1)} all-gather(bf16[48,384]{1,0:T(8,128)(2,1)S(1)} %convert_element_type.142), channel_id=1, replica_groups=mesh['dp'=16,'mp'=2] {'dp'}, dimensions={0}, use_global_device_ids=true | all-gather | bytes 626688 | tf_op jit(solution)/shard_map/all_gather | solution.py:91
  127.3 111.0 %while.28 = (s32[]{:T(128)}, bf16[3,512,8,48]{1,3,2,0:T(8,128)(2,1)}, f32[3,8,512]{2,1,0:T(8,128)}, s32[3,512]{1,0:T(4,128)}, s32[1536]{0:T(1024)S(1)}, /*index=...) while((s32[]{:T(128)}, ...), condition=%wide.region_6.7_spmd.clone, body=%wide.region_3.6_spmd.clone.sunk | while | flops 1285812224 | bytes 91769016 | solution.py:142
  255.7 29.9 %all-reduce.5 = (bf16[768]{0:T(1024)(128)(2,1)}, bf16[768]{0:T(1024)(128)(2,1)}) all-reduce(bf16[768]{0:T(1024)(128)(2,1)S(1)} %dynamic-update-slice, bf16[768]{0:T(1024)(128)(2,1)S(1)} %dynamic-update-slice.1), channel_id=1, replica_groups=mesh['dp'=16,'mp'=2] {'dp'}, use_global_device_ids=true, to_apply=%add | all-reduce | flops 1536 | bytes 6144
  286.9 25.5 %all-reduce.11.cloned.1.call-done = bf16[1536,768]{1,0:T(8,128)(2,1)} async-done(((bf16[1536,768]{1,0:T(8,128)(2,1)}), bf16[1536,768]{1,0:T(8,128)(2,1)}) %all-reduce.11.cloned.1.call-update) | async-done | bytes 2359312 | tf_op jit(solution)/shard_map/psum | solution.py:147
  331.6 12.7 multiply_convert_fusion.3
  344.3 30.2 %all-gather.8.cloned.1.call-done = bf16[1280,768]{0,1:T(8,128)(2,1)} async-done(((bf16[1280,48]{0,1:T(8,128)(2,1)}), bf16[1280,768]{0,1:T(8,128)(2,1)}) %all-gather.8.cloned.1.call-update) | async-done | bytes 1966096 | tf_op jit(solution)/shard_map/all_gather | solution.py:100
  383.3 65.8 %all-reduce.13.cloned.1.call-done = bf16[1536,768]{1,0:T(8,128)(2,1)} async-done(((bf16[1536,768]{1,0:T(8,128)(2,1)}), bf16[1536,768]{1,0:T(8,128)(2,1)}) %all-reduce.13.cloned.1.call-update) | async-done | bytes 2359312 | tf_op jit(solution)/shard_map/psum | solution.py:160
  480.9 68.7 %all-reduce.15.cloned.1.call-done = bf16[1536,768]{1,0:T(8,128)(2,1)} async-done(((bf16[1536,768]{1,0:T(8,128)(2,1)}), bf16[1536,768]{1,0:T(8,128)(2,1)}) %all-reduce.15.cloned.1.call-update) | async-done | bytes 2359312 | tf_op jit(solution)/shard_map/psum | solution.py:182
  573.8 328.7 %while.29 = (s32[]{:T(128)}, f32[1536,8,48]{0,2,1:T(8,128)S(1)}, f32[1536,8,48]{0,2,1:T(8,128)}, f32[3,512,8,48]{1,0,3,2:T(4,128)}, bf16[3,512,8,48]{1,3,2,0:T(8...) while((s32[]{:T(128)}, f32[1536,8,48]{0,2,1:T(8,128)S(1)}, ...), condition=%wide.region_16.17_spmd.clone, body=%wide.region_14.16_spmd.clone.sunk | while | flops 3082022912 | bytes 212093184 | solution.py:227
  578.0 13.2 fusion.152
  591.1 24.3 %multiply_reduce_fusion.6 = (f32[8,512]{1,0:T(8,128)S(1)}, f32[8,512,1536]{2,1,0:T(8,128)}) fusion(f32[8,512,1536]{2,1,0:T(8,128)} %fusion.152, f32[8,512]{1,0:T(8,128)} %dynamic-slice_bitcast_fusion.2, bf16[1536,8,48]{0,2,1:T(8,128)(2,1)S(1)} %get-tuple-element.612, bf16[3,512,8,48]{1,3,2,0:T(8,128)(2,1)} %get-tuple-element.608, s32[]{:T(128)S(6)} %copy.99, ...), kind=kOutput, calls=%fused_computation.22.clone.1 | convolution fusion | flops 635432960 | bytes 52723716 | tf_op jit(solution)/shard_map/while/body/eval_jaxpr/qhd,khd->hqk/dot_general | solution.py:67
  615.5 21.4 %multiply_convert_fusion.7 = bf16[8,512,1536]{2,1,0:T(8,128)(2,1)} fusion(f32[8,512,1536]{2,1,0:T(8,128)} %get-tuple-element.544, f32[8,512,1536]{2,1,0:T(8,128)} %fusion.152, f32[8,512]{1,0:T(8,128)S(1)} %get-tuple-element.545), kind=kLoop, calls=%fused_computation.21.clone.1 | loop fusion | flops 18874368 | bytes 62930944 | tf_op jit(solution)/shard_map/while/body/eval_jaxpr/convert_element_type | solution.py:206
  667.0 16.1 %dynamic_update_slice.21 = f32[3,512,8,48]{1,0,3,2:T(4,128)} dynamic-update-slice(f32[3,512,8,48]{1,0,3,2:T(4,128)} %get-tuple-element.593, f32[1,512,8,48]{1,0,3,2:T(1,128)} %copy.77, s32[]{:T(128)S(6)} %copy.99, s32[]{:T(128)} %constant.60.clone.1..sunk, s32[]{:T(128)} %constant.60.clone.1..sunk, s32[]{:T(128)} %constant.60.clone.1..sunk) | dynamic-update-slice | bytes 1572868 | tf_op jit(solution)/shard_map/while/body/jit(dynamic_update_index_in_dim)/dynamic_update_slice | solution.py:142
  686.9 13.2 fusion.152
  700.0 24.4 %multiply_reduce_fusion.6 = (f32[8,512]{1,0:T(8,128)S(1)}, f32[8,512,1536]{2,1,0:T(8,128)}) fusion(f32[8,512,1536]{2,1,0:T(8,128)} %fusion.152, f32[8,512]{1,0:T(8,128)} %dynamic-slice_bitcast_fusion.2, bf16[1536,8,48]{0,2,1:T(8,128)(2,1)S(1)} %get-tuple-element.612, bf16[3,512,8,48]{1,3,2,0:T(8,128)(2,1)} %get-tuple-element.608, s32[]{:T(128)S(6)} %copy.99, ...), kind=kOutput, calls=%fused_computation.22.clone.1 | convolution fusion | flops 635432960 | bytes 52723716 | tf_op jit(solution)/shard_map/while/body/eval_jaxpr/qhd,khd->hqk/dot_general | solution.py:67
  724.4 21.4 %multiply_convert_fusion.7 = bf16[8,512,1536]{2,1,0:T(8,128)(2,1)} fusion(f32[8,512,1536]{2,1,0:T(8,128)} %get-tuple-element.544, f32[8,512,1536]{2,1,0:T(8,128)} %fusion.152, f32[8,512]{1,0:T(8,128)S(1)} %get-tuple-element.545), kind=kLoop, calls=%fused_computation.21.clone.1 | loop fusion | flops 18874368 | bytes 62930944 | tf_op jit(solution)/shard_map/while/body/eval_jaxpr/convert_element_type | solution.py:206
  745.8 12.7 fusion.155
  776.6 16.1 %dynamic_update_slice.21 = f32[3,512,8,48]{1,0,3,2:T(4,128)} dynamic-update-slice(f32[3,512,8,48]{1,0,3,2:T(4,128)} %get-tuple-element.593, f32[1,512,8,48]{1,0,3,2:T(1,128)} %copy.77, s32[]{:T(128)S(6)} %copy.99, s32[]{:T(128)} %constant.60.clone.1..sunk, s32[]{:T(128)} %constant.60.clone.1..sunk, s32[]{:T(128)} %constant.60.clone.1..sunk) | dynamic-update-slice | bytes 1572868 | tf_op jit(solution)/shard_map/while/body/jit(dynamic_update_index_in_dim)/dynamic_update_slice | solution.py:142
  796.5 13.2 fusion.152
  809.6 24.4 %multiply_reduce_fusion.6 = (f32[8,512]{1,0:T(8,128)S(1)}, f32[8,512,1536]{2,1,0:T(8,128)}) fusion(f32[8,512,1536]{2,1,0:T(8,128)} %fusion.152, f32[8,512]{1,0:T(8,128)} %dynamic-slice_bitcast_fusion.2, bf16[1536,8,48]{0,2,1:T(8,128)(2,1)S(1)} %get-tuple-element.612, bf16[3,512,8,48]{1,3,2,0:T(8,128)(2,1)} %get-tuple-element.608, s32[]{:T(128)S(6)} %copy.99, ...), kind=kOutput, calls=%fused_computation.22.clone.1 | convolution fusion | flops 635432960 | bytes 52723716 | tf_op jit(solution)/shard_map/while/body/eval_jaxpr/qhd,khd->hqk/dot_general | solution.py:67
  834.0 21.4 %multiply_convert_fusion.7 = bf16[8,512,1536]{2,1,0:T(8,128)(2,1)} fusion(f32[8,512,1536]{2,1,0:T(8,128)} %get-tuple-element.544, f32[8,512,1536]{2,1,0:T(8,128)} %fusion.152, f32[8,512]{1,0:T(8,128)S(1)} %get-tuple-element.545), kind=kLoop, calls=%fused_computation.21.clone.1 | loop fusion | flops 18874368 | bytes 62930944 | tf_op jit(solution)/shard_map/while/body/eval_jaxpr/convert_element_type | solution.py:206
  886.2 16.1 %dynamic_update_slice.21 = f32[3,512,8,48]{1,0,3,2:T(4,128)} dynamic-update-slice(f32[3,512,8,48]{1,0,3,2:T(4,128)} %get-tuple-element.593, f32[1,512,8,48]{1,0,3,2:T(1,128)} %copy.77, s32[]{:T(128)S(6)} %copy.99, s32[]{:T(128)} %constant.60.clone.1..sunk, s32[]{:T(128)} %constant.60.clone.1..sunk, s32[]{:T(128)} %constant.60.clone.1..sunk) | dynamic-update-slice | bytes 1572868 | tf_op jit(solution)/shard_map/while/body/jit(dynamic_update_index_in_dim)/dynamic_update_slice | solution.py:142
  969.4 30.3 %all-reduce.4 = (f32[768]{0:T(1024)S(1)}, f32[768]{0:T(1024)S(1)}) all-reduce(f32[768]{0:T(1024)S(1)} %copy-done.49, f32[768]{0:T(1024)S(1)} %copy-done.50), channel_id=6, replica_groups=mesh['dp'=16,'mp'=2] {'dp'}, use_global_device_ids=true, to_apply=%region_23.24.clone | all-reduce | flops 1536 | bytes 12288
  1006.8 38.8 %reduce-scatter.26.cloned.1.call-done = f32[48,384]{1,0:T(8,128)} async-done(((f32[768,384]{1,0:T(8,128)}), f32[48,384]{1,0:T(8,128)}) %reduce-scatter.26.cloned.1.call-update) | async-done | bytes 73744
  1045.6 61.2 %reduce-scatter.24.cloned.1.call-done = f32[48,384]{1,0:T(8,128)} async-done(((f32[768,384]{1,0:T(8,128)}), f32[48,384]{1,0:T(8,128)}) %reduce-scatter.24.cloned.1.call-update) | async-done | bytes 73744
  1106.8 61.1 %reduce-scatter.22.cloned.1.call-done = f32[48,384]{1,0:T(8,128)} async-done(((f32[768,384]{1,0:T(8,128)}), f32[48,384]{1,0:T(8,128)}) %reduce-scatter.22.cloned.1.call-update) | async-done | bytes 73744
  1167.9 74.2 %reduce-scatter.20.cloned.1.call-done = f32[1280,48]{0,1:T(8,128)} async-done(((f32[1280,768]{0,1:T(8,128)}), f32[1280,48]{0,1:T(8,128)}) %reduce-scatter.20.cloned.1.call-update) | async-done | bytes 245776 | tf_op jit(solution)/shard_map/reduce_scatter | solution.py:265
  1242.1 73.8 %reduce-scatter.16.cloned.1.call-done = f32[48,1280]{1,0:T(8,128)} async-done(((f32[768,1280]{1,0:T(8,128)}), f32[48,1280]{1,0:T(8,128)}) %reduce-scatter.16.cloned.1.call-update) | async-done | bytes 245776 | tf_op jit(solution)/shard_map/reduce_scatter | solution.py:263
  1315.9 73.9 %reduce-scatter.18.cloned.1.call-done = f32[48,1280]{1,0:T(8,128)} async-done(((f32[768,1280]{1,0:T(8,128)}), f32[48,1280]{1,0:T(8,128)}) %reduce-scatter.18.cloned.1.call-update) | async-done | bytes 245776 | tf_op jit(solution)/shard_map/reduce_scatter | solution.py:264
  (298 shorter events, 410.0 us)
Async XLA Ops:
  8.0 304.4 %all-reduce.11.cloned.1.call-start = ((), (), s32[]{:S(2)}) async-start(), calls=%async_computation.7 | async-start | bytes 4718592 | tf_op jit(solution)/shard_map/psum | solution.py:147
  10.4 92.6 %copy-start.3 = (bf16[1536,768]{1,0:T(8,128)(2,1)S(1)}, bf16[1536,768]{1,0:T(8,128)(2,1)}, u32[]{:S(2)}) copy-start(bf16[1536,768]{1,0:T(8,128)(2,1)} %param.16) | copy-start | bytes 7077892
  63.5 40.6 %copy-start.30 = (bf16[768,384]{1,0:T(8,128)(2,1)}, bf16[768,384]{1,0:T(8,128)(2,1)S(1)}, u32[]{:S(2)}) copy-start(bf16[768,384]{1,0:T(8,128)(2,1)S(1)} %all_gather.29) | copy-start | bytes 1769476
  84.0 22.8 %copy-start.32 = (bf16[768,384]{1,0:T(8,128)(2,1)}, bf16[768,384]{1,0:T(8,128)(2,1)S(1)}, u32[]{:S(2)}) copy-start(bf16[768,384]{1,0:T(8,128)(2,1)S(1)} %all_gather.28) | copy-start | bytes 1769476
  139.7 11.9 copy-start.41
  176.5 11.9 copy-start.41
  213.4 11.9 copy-start.41
  245.7 66.7 %copy-start.4 = (bf16[1536,768]{1,0:T(8,128)(2,1)S(1)}, bf16[1536,768]{1,0:T(8,128)(2,1)}, u32[]{:S(2)}) copy-start(bf16[1536,768]{1,0:T(8,128)(2,1)} %param.16) | copy-start | bytes 7077892
  245.7 71.7 %all-gather.4.cloned.1.call-start = ((), (), s32[]{:S(2)}) async-start(), calls=%async_computation.8 | async-start | bytes 2088960 | tf_op jit(solution)/shard_map/all_gather | solution.py:98
  247.6 84.1 %all-gather.6.cloned.1.call-start = ((), (), s32[]{:S(2)}) async-start(), calls=%async_computation.9 | async-start | bytes 2088960 | tf_op jit(solution)/shard_map/all_gather | solution.py:99
  249.3 125.3 %all-gather.8.cloned.1.call-start = ((), (), s32[]{:S(2)}) async-start(), calls=%async_computation.10 | async-start | bytes 2088960 | tf_op jit(solution)/shard_map/all_gather | solution.py:100
  251.1 198.1 %all-reduce.13.cloned.1.call-start = ((), (), s32[]{:S(2)}) async-start(), calls=%async_computation.11 | async-start | bytes 4718592 | tf_op jit(solution)/shard_map/psum | solution.py:160
  382.0 167.7 %all-reduce.15.cloned.1.call-start = ((), (), s32[]{:S(2)}) async-start(), calls=%async_computation.12 | async-start | bytes 4718592 | tf_op jit(solution)/shard_map/psum | solution.py:182
  457.8 11.6 copy-start.10
  457.8 11.6 copy-start.52
  480.9 520.1 %all-reduce.17.cloned.1.call-start = ((), (), s32[]{:S(2)}) async-start(), calls=%async_computation.13 | async-start | bytes 4718592 | tf_op jit(solution)/shard_map/psum | solution.py:254
  549.7 7.2 copy-start.11
  549.7 7.9 copy-start.15
  549.7 7.9 copy-start.46
  658.1 7.1 copy-start
  665.2 17.8 %copy-start.40 = (s32[1536]{0:T(1024)S(1)}, s32[1536]{0:T(1024)}, u32[]{:S(2)}) copy-start(s32[1536]{0:T(1024)} %copy-done.39) | copy-start | bytes 18436 | tf_op jit(solution)/shard_map/while
  767.7 7.1 copy-start
  774.8 17.8 %copy-start.40 = (s32[1536]{0:T(1024)S(1)}, s32[1536]{0:T(1024)}, u32[]{:S(2)}) copy-start(s32[1536]{0:T(1024)} %copy-done.39) | copy-start | bytes 18436 | tf_op jit(solution)/shard_map/while
  884.5 17.8 %copy-start.40 = (s32[1536]{0:T(1024)S(1)}, s32[1536]{0:T(1024)}, u32[]{:S(2)}) copy-start(s32[1536]{0:T(1024)} %copy-done.39) | copy-start | bytes 18436 | tf_op jit(solution)/shard_map/while
  904.3 15.3 %copy-start.23 = (bf16[1536,8,48]{0,2,1:T(8,128)(2,1)}, bf16[1536,8,48]{0,2,1:T(8,128)(2,1)S(1)}, u32[]{:S(2)}) copy-start(bf16[1536,8,48]{0,2,1:T(8,128)(2,1)S(1)} %convert_element_type.178) | copy-start | bytes 3538948
  922.7 84.1 %reduce-scatter.14.cloned.1.call-start = ((), (), s32[]{:S(2)}) async-start(), calls=%async_computation.14 | async-start | bytes 1253376 | tf_op jit(solution)/shard_map/reduce_scatter | solution.py:261
  928.1 117.5 %reduce-scatter.26.cloned.1.call-start = ((), (), s32[]{:S(2)}) async-start(), calls=%async_computation.20 | async-start | bytes 1253376
  933.0 173.8 %reduce-scatter.24.cloned.1.call-start = ((), (), s32[]{:S(2)}) async-start(), calls=%async_computation.19 | async-start | bytes 1253376
  938.1 229.8 %reduce-scatter.22.cloned.1.call-start = ((), (), s32[]{:S(2)}) async-start(), calls=%async_computation.18 | async-start | bytes 1253376
  943.2 298.9 %reduce-scatter.20.cloned.1.call-start = ((), (), s32[]{:S(2)}) async-start(), calls=%async_computation.17 | async-start | bytes 4177920 | tf_op jit(solution)/shard_map/reduce_scatter | solution.py:265
  952.2 363.7 %reduce-scatter.16.cloned.1.call-start = ((), (), s32[]{:S(2)}) async-start(), calls=%async_computation.15 | async-start | bytes 4177920 | tf_op jit(solution)/shard_map/reduce_scatter | solution.py:263
  961.2 428.7 %reduce-scatter.18.cloned.1.call-start = ((), (), s32[]{:S(2)}) async-start(), calls=%async_computation.16 | async-start | bytes 4177920 | tf_op jit(solution)/shard_map/reduce_scatter | solution.py:264
  (49 other events, 154.3 us)
Sparse Core Ops, SparseCore 0:
  245.9 66.4 all-reduce.10
  382.1 67.0 all-reduce.12
  481.0 68.6 all-reduce.14
  922.8 68.6 all-reduce.16
Sparse Core Ops, SparseCore 1:
  249.3 39.4 all-gather.3
  291.8 39.8 all-gather.5
  334.6 39.8 all-gather.7
  928.1 56.4 reduce-scatter.13
  988.9 56.7 reduce-scatter.25
  1049.8 57.0 reduce-scatter.23
  1110.9 56.9 reduce-scatter.21
  1172.2 69.8 reduce-scatter.19
  1246.9 68.9 reduce-scatter.15
  1320.4 69.4 reduce-scatter.17
where the time goes:
time: 1410 us; the launch traced here: 1400 us
  waiting for transfers between devices  579 us (41%)
  matrix products  369 us (26%)
  other arithmetic  168 us (12%)
  blocking collectives  145 us (10%)
  local copies, waits for them, and re-layouts  117 us (8%)
  between operations  17.6 us (1%)
    unnamed x17, waiting for transfers between devices  161 us
    dot_general x6, matrix products, masked_scores(): jnp.einsum('qhd,khd->hqk', query_block, key_rot, preferred_element_type=j...  105 us
    reduce_scatter x1, waiting for transfers between devices, on_device(): lax.psum_scatter(grad_down, 'dp', scatter_dimension=1, tiled=True)  74.2 us
    reduce_scatter x1, waiting for transfers between devices, on_device(): lax.psum_scatter(grad_up, 'dp', scatter_dimension=0, tiled=True)  73.9 us
    reduce_scatter x1, waiting for transfers between devices, on_device(): lax.psum_scatter(grad_gate, 'dp', scatter_dimension=0, tiled=True)  73.8 us
    psum x1, waiting for transfers between devices, on_device(): lax.psum(hidden_term.astype(jnp.bfloat16), 'mp').astype(jnp.float32)  68.7 us
    psum x1, waiting for transfers between devices, on_device(): ffn_total = lax.psum(ffn_part, 'mp').astype(jnp.float32)  65.8 us
    convert_element_type x3, other arithmetic, backward_block(): grad_scores = (soft_probs * (grad_probs - row_dot)).astype(jnp.bfloat16)  64.2 us
  transfers between devices with their start and end apart: 14, of which 11 were waited for; matrix products, arithmetic and copies ran while one was open for 6% of the time, Pallas kernels for 0%

commit v1 on v0

v1 whole, which is shorter than its diff:
```python
import functools, math
import jax, jax.numpy as jnp
from jax import lax
from jax.experimental import pallas as pl
from jax.experimental.pallas import tpu as pltpu
HD=48
C2=HD**-0.5*math.log2(math.e)
NEG=-1e30
bf=jnp.bfloat16; f32=jnp.float32
QB=256; LOOK=4
NT=(((1,),(1,)),((),()))
def dot(a,b): return jnp.dot(a,b,preferred_element_type=f32)
def dot_nt(a,b): return lax.dot_general(a,b,NT,preferred_element_type=f32)

def spread(rows, cols, rot):
    r=lax.broadcasted_iota(jnp.int32,(rows,cols),0); c=lax.broadcasted_iota(jnp.int32,(rows,cols),1)
    h=r//64; d=r-h*64
    if not rot:
        return jnp.where((d<HD)&(c==h*HD+d),1.0,0.0).astype(bf)
    lo=(d<24)&(c==h*HD+d+24); hi=(d>=24)&(d<HD)&(c==h*HD+d-24)
    return jnp.where(lo,-1.0,jnp.where(hi,1.0,0.0)).astype(bf)

def proj(tok,w,cos,sin,wq_s,q_s,k_s,v_s,n,cols):
    hp=cols//HD*64
    pairs=hp//128
    for m,(col,rot) in enumerate(((0,False),(0,True),(1,False),(1,True),(2,False))):
        wq_s[m]=dot_nt(spread(hp,cols,rot),w[:,col*cols:(col+1)*cols]).astype(bf)
    def body(b,_):
        rows=pl.ds(pl.multiple_of(b*QB,QB),QB)
        x=tok[rows,:]
        cs=cos[rows,:]; sn=sin[rows,:]
        for dst,a in ((q_s,0),(k_s,2)):
            raw=dot_nt(x,wq_s[a]); rt=dot_nt(x,wq_s[a+1])
            for p in range(pairs):
                l=slice(p*128,p*128+128)
                dst[p,rows,:]=(raw[:,l]*cs+rt[:,l]*sn).astype(bf)
        raw=dot_nt(x,wq_s[4])
        for p in range(pairs):
            v_s[p,rows,:]=raw[:,p*128:p*128+128].astype(bf)
        return 0
    lax.fori_loop(0,n//QB,body,0)

def masks(kk0,nk,i,start):
    kidx=lax.broadcasted_iota(jnp.int32,(nk,QB),0)+kk0
    ok=kidx>=start
    qidx=lax.broadcasted_iota(jnp.int32,(nk,QB),1)+i*QB
    return ok&(kidx<=qidx)

def fwd_head(h,i,q_t,k_s,v_t,start,m_t,lse):
    p=h//2; half=h-2*p
    lo=max(0,i-LOOK)*QB; nk=(i+1)*QB-lo
    kk=slice(lo,lo+nk); qq=slice(i*QB,(i+1)*QB)
    row=lax.broadcasted_iota(jnp.int32,(128,QB),0)
    mine=(row>=half*64)&(row<half*64+64)
    qt=jnp.where(mine,q_t[p,:,qq],jnp.zeros((),bf))
    s=dot(k_s[p,kk,:],qt)
    st=start[:,qq]
    s=jnp.where(masks(lo,nk,i,st),s,NEG)
    m=jnp.max(s,0,keepdims=True)
    e=jnp.exp2((s-m)*C2)
    l=jnp.sum(e,0,keepdims=True)
    pr=(e*(1.0/l)).astype(bf)
    rows=pl.ds(pl.multiple_of(half*64,64),64)
    m_t[p,rows,qq]=dot(v_t[p,rows,kk],pr)
    lse[pl.ds(h,1),qq]=m*C2+jnp.log2(l)

def fwd_kernel(n,cols,tok,w,cos,sin,start,q_o,k_o,v_o,m_t,mixed,lse,wq_s,q_t,v_t):
    proj(tok,w,cos,sin,wq_s,q_o,k_o,v_o,n,cols)
    heads=cols//HD
    for p in range(heads//2):
        q_t[p]=q_o[p].T
        v_t[p]=v_o[p].T
    def body(h,_):
        for i in range(n//QB):
            fwd_head(h,i,q_t,k_o,v_t,start,m_t,lse)
        return 0
    lax.fori_loop(0,heads,body,0)
    for p in range(heads//2):
        mixed[:,p*128:p*128+128]=m_t[p].T.astype(bf)

def attn_fwd(tok,w,cos,sin,start):
    n=tok.shape[0]; cols=w.shape[1]//3; heads=cols//HD; P=heads//2
    V=pl.BlockSpec(memory_space=pltpu.VMEM)
    S=jax.ShapeDtypeStruct
    return pl.pallas_call(functools.partial(fwd_kernel,n,cols),
      out_shape=(S((P,n,128),bf),S((P,n,128),bf),S((P,n,128),bf),S((P,128,n),f32),S((n,P*128),bf),S((heads,n),f32)),
      in_specs=[V]*5,out_specs=[V]*6,
      scratch_shapes=[pltpu.VMEM((5,P*128,w.shape[0]),bf),pltpu.VMEM((P,128,n),bf),pltpu.VMEM((P,128,n),bf)],
      compiler_params=pltpu.CompilerParams(vmem_limit_bytes=60<<20),name="attn_fwd")(tok,w,cos,sin,start)

def bwd_head(h,i,q_t,q_s,k_s,k_t,v_s,dm_t,dm_s,lse,dd,start,dq_t,dk_s,dv_s):
    p=h//2; half=h-2*p
    lo=max(0,i-LOOK)*QB; nk=(i+1)*QB-lo
    kk=slice(lo,lo+nk); qq=slice(i*QB,(i+1)*QB)
    row=lax.broadcasted_iota(jnp.int32,(128,QB),0)
    mine=(row>=half*64)&(row<half*64+64)
    lane=lax.broadcasted_iota(jnp.int32,(QB,128),1)
    mlane=(lane>=half*64)&(lane<half*64+64)
    zero=jnp.zeros((),bf)
    qt=jnp.where(mine,q_t[p,:,qq],zero)
    dmt=jnp.where(mine,dm_t[p,:,qq],zero)
    qn=jnp.where(mlane,q_s[p,qq,:],zero)
    dmn=jnp.where(mlane,dm_s[p,qq,:],zero)
    s=dot(k_s[p,kk,:],qt)
    st=start[:,qq]
    pr=jnp.exp2(jnp.where(masks(lo,nk,i,st),s*C2,NEG)-lse[pl.ds(h,1),qq])
    dp=dot(v_s[p,kk,:],dmt)
    ds=(pr*(dp-dd[pl.ds(h,1),qq])).astype(bf)
    pb=pr.astype(bf)
    dv_s[p,kk,:]+=dot(pb,dmn)
    dk_s[p,kk,:]+=dot(ds,qn)
    rows=pl.ds(pl.multiple_of(half*64,64),64)
    dq_t[p,rows,qq]=dot(k_t[p,rows,kk],ds)

def rope_back(u,cs,sn):
    w=u*sn
    lane=lax.broadcasted_iota(jnp.int32,u.shape,1)&63
    up=pltpu.roll(w,128-24,axis=1); dn=pltpu.roll(w,24,axis=1)
    return u*cs+jnp.where(lane<24,up,jnp.where(lane<48,-dn,0.0))

def bwd_kernel(n,heads,q_s,k_s,v_s,m_t,dm,lse,start,cos,sin,dqkv,q_t,k_t,dm_t,dm_s,dq_t,dk_s,dv_s,dd):
    P=heads//2
    for p in range(P):
        q_t[p]=q_s[p].T
        k_t[p]=k_s[p].T
        dm_s[p]=dm[:,p*128:p*128+128]
        dm_t[p]=dm_s[p].T
        for half in range(2):
            r=slice(half*64,half*64+64)
            dd[2*p+half:2*p+half+1,:]=jnp.sum(dm_t[p,r,:].astype(f32)*m_t[p,r,:],0,keepdims=True)
    dk_s[...]=jnp.zeros_like(dk_s); dv_s[...]=jnp.zeros_like(dv_s)
    def body(h,_):
        for i in range(n//QB):
            bwd_head(h,i,q_t,q_s,k_s,k_t,v_s,dm_t,dm_s,lse,dd,start,dq_t,dk_s,dv_s)
        return 0
    lax.fori_loop(0,heads,body,0)
    sc=HD**-0.5
    for p in range(P):
        dqkv[0,:,p*128:p*128+128]=rope_back(dq_t[p].T*sc,cos[...],sin[...]).astype(bf)
        dqkv[1,:,p*128:p*128+128]=rope_back(dk_s[p]*sc,cos[...],sin[...]).astype(bf)
        dqkv[2,:,p*128:p*128+128]=dv_s[p].astype(bf)

def attn_bwd(q_s,k_s,v_s,m_t,dm,lse,start,cos,sin):
    P,n,_=q_s.shape; heads=2*P
    V=pl.BlockSpec(memory_space=pltpu.VMEM)
    S=jax.ShapeDtypeStruct
    return pl.pallas_call(functools.partial(bwd_kernel,n,heads),
      out_shape=S((3,n,P*128),bf),
      in_specs=[V]*9,out_specs=V,
      scratch_shapes=[pltpu.VMEM((P,128,n),bf),pltpu.VMEM((P,128,n),bf),pltpu.VMEM((P,128,n),bf),pltpu.VMEM((P,n,128),bf),pltpu.VMEM((P,128,n),f32),pltpu.VMEM((P,n,128),f32),pltpu.VMEM((P,n,128),f32),pltpu.VMEM((heads,n),f32)],
      compiler_params=pltpu.CompilerParams(vmem_limit_bytes=60<<20),name="attn_bwd")(q_s,k_s,v_s,m_t,dm,lse,start,cos,sin)


from jax.sharding import Mesh, PartitionSpec as P

NORM_EPS=1e-05
DIAG=[(0,0),(3,3),(1,2),(2,1)]
CORE=[(0,1),(1,0)]

def rms_forward(resid):
    inverse=lax.rsqrt(jnp.mean(resid*resid,-1,keepdims=True)+NORM_EPS)
    return (resid*inverse,inverse)

def rms_backward(grad_normed,normed,inverse):
    return inverse*(grad_normed-normed*jnp.mean(grad_normed*normed,-1,keepdims=True))

def doc_starts(lengths,n):
    at=jnp.arange(n,dtype=jnp.int32); start=jnp.zeros((n,),jnp.int32); end=jnp.int32(0)
    for i in range(lengths.shape[0]-1):
        end=end+lengths[i]
        start=jnp.where(at>=end,end,start)
    return start

def rope_tables(positions):
    half=HD//2
    fr=jnp.exp(jnp.arange(half,dtype=f32)*(-2.0*math.log(10000.0)/HD))
    a=positions.astype(f32)[:,None]*fr[None,:]
    c,s=jnp.cos(a),jnp.sin(a); z=jnp.zeros((positions.shape[0],64-HD),f32)
    return jnp.concatenate([c,c,z,c,c,z],1),jnp.concatenate([s,s,z,s,s,z],1)

def core_sum(part):
    return part.astype(f32)+lax.ppermute(part,"c",CORE).astype(f32)

def on_device(tokens,out_grad,doc_lengths,w_query,w_key,w_value,w_out,gain_one,w_gate,w_up,w_down,gain_two):
    own=lax.axis_index("c")==lax.axis_index("m")
    pick=lambda a: jnp.where(own,a,lax.ppermute(a,"c",CORE))
    tokens,out_grad,doc_lengths=pick(tokens),pick(out_grad),pick(doc_lengths)
    cast=lambda a: a.astype(bf)
    gains=jnp.pad(jnp.stack([cast(gain_one),cast(gain_two)],1),((0,0),(0,126)))
    apack=jnp.concatenate([cast(w_query),cast(w_key),cast(w_value),cast(w_out).T,gains],1)
    fpack=jnp.concatenate([cast(w_gate),cast(w_up),cast(w_down).T],1)
    def gather(a):
        return lax.all_gather(lax.ppermute(a,("c","m"),DIAG),("q","m"),axis=0,tiled=True)
    afull,ffull=gather(apack),gather(fpack)
    cols=w_query.shape[1]; ff=w_gate.shape[1]; n,width=tokens.shape
    hp=cols//HD*64
    put=spread(hp,cols,False)
    out_t=dot_nt(afull[:,3*cols:4*cols],put).astype(bf)
    gain_a=afull[:,4*cols].astype(f32); gain_b=afull[:,4*cols+1].astype(f32)
    gate_w,up_w,down_t=ffull[:,:ff],ffull[:,ff:2*ff],ffull[:,2*ff:]
    start=doc_starts(doc_lengths[0],n)
    cos,sin=rope_tables(jnp.arange(n,dtype=jnp.int32)-start)
    start=start[None]
    q,k,v,m_t,mixed,lse=attn_fwd(tokens,afull[:,:3*cols],cos,sin,start)
    attn=core_sum(dot_nt(mixed,out_t).astype(bf))
    normed_one,inv_one=rms_forward(tokens.astype(f32)+attn)
    hidden=normed_one*gain_a
    hb=hidden.astype(bf)
    gate=dot(hb,gate_w); up=dot(hb,up_w)
    sg=jax.nn.sigmoid(gate)
    act=(gate*sg*up).astype(bf)
    ffn=core_sum(dot_nt(act,down_t).astype(bf))
    normed_two,inv_two=rms_forward(hidden+ffn)
    output=(normed_two*gain_b).astype(bf)
    g=out_grad.astype(f32)
    g_gain_two=jnp.sum(g*normed_two,0)
    d_two=rms_backward(g*gain_b,normed_two,inv_two)
    d_ffn=d_two.astype(bf)
    tn=lambda a,b: lax.dot_general(a,b,(((0,),(0,)),((),())),preferred_element_type=f32)
    d_act=dot(d_ffn,down_t)
    d_up=(d_act*gate*sg).astype(bf)
    d_gate=(d_act*up*sg*(1.0+gate*(1.0-sg))).astype(bf)
    hterm=(dot_nt(d_gate,gate_w)+dot_nt(d_up,up_w)).astype(bf)
    gff=jnp.concatenate([tn(hb,d_gate).astype(bf),tn(hb,d_up).astype(bf),tn(d_ffn,act).astype(bf)],1)
    d_hidden=d_two+core_sum(hterm)
    g_gain_one=jnp.sum(d_hidden*normed_one,0)
    d_one=rms_backward(d_hidden*gain_a,normed_one,inv_one)
    d_attn=d_one.astype(bf)
    g_out=dot(tn(d_attn,mixed).astype(bf),put).astype(bf)
    dm=dot(d_attn,out_t).astype(bf)
    dqkv=attn_bwd(q,k,v,m_t,dm,lse,start,cos,sin)
    term=0.0; gqkv=[]
    for j in range(3):
        wp=dot_nt(afull[:,j*cols:(j+1)*cols],put).astype(bf)
        term=term+dot_nt(dqkv[j],wp)
        gqkv.append(dot(tn(tokens,dqkv[j]).astype(bf),put).astype(bf))
    gtok=(d_one+core_sum(term.astype(bf))).astype(bf)
    ggain=jnp.pad(jnp.stack([g_gain_one,g_gain_two],1),((0,0),(0,126))).astype(bf)
    gatt=jnp.concatenate(gqkv+[g_out,ggain],1)
    def scatter(a):
        return lax.ppermute(lax.psum_scatter(a,("q","m"),scatter_dimension=0,tiled=True),("c","m"),DIAG).astype(f32)
    sff,sat=scatter(gff),scatter(gatt)
    output=lax.ppermute(output,("c","m"),DIAG)
    gtok=lax.ppermute(gtok,("c","m"),DIAG).astype(f32)
    return (output,gtok,sat[:,:cols],sat[:,cols:2*cols],sat[:,2*cols:3*cols],sat[:,3*cols:4*cols].T,sat[:,4*cols],
            sff[:,:ff],sff[:,ff:2*ff],sff[:,2*ff:].T,sat[:,4*cols+1])

def solution(mesh):
    dp,mp=mesh.shape["dp"],mesh.shape["mp"]
    fine=Mesh(mesh.devices.reshape(dp//2,2,mp),("q","c","m"))
    d=("q","c")
    rows,cols_=P(d,"m"),P("m",d)
    return jax.shard_map(on_device,mesh=fine,
        in_specs=(P(d,None),P(d,None),P(d,None),rows,rows,rows,cols_,P(d),rows,rows,cols_,P(d)),
        out_specs=(P(d,None),P(d,None),rows,rows,rows,cols_,P(d),rows,rows,cols_,P(d)),check_vma=False)
```

time: 1410 us -> 622 us (0.44)
  waiting for transfers between devices: 579 us -> 301 us
  matrix products: 369 us -> 99.1 us
  blocking collectives: 145 us -> 0 us
  other arithmetic: 168 us -> 41.6 us
  Pallas kernels: 0 us -> 91.5 us
  local copies, waits for them, and re-layouts: 117 us -> 30.4 us
  starting transfers between devices: 0.82 us -> 30.2 us
    dot_general x42 -> x19, matrix products: 369 us -> 99.1 us  [the longest x8 48.6 us: dot(): return jnp.dot(a, b, preferred_element_type=f32)]
    psum x4 -> x0, waiting for transfers between devices: 160 us -> none  [the longest x1 68.7 us: on_device(): lax.psum(hidden_term.astype(jnp.bfloat16), 'mp').astype(jnp.float32)]
    pallas_call x0 -> x2, Pallas kernels: none -> 91.5 us  [the longest x1 50.6 us: attn_fwd(): pl.pallas_call(functools.partial(fwd_kernel, n, cols), out_shape=(S((P, n...]
    reduce_scatter x4 -> x1, waiting for transfers between devices: 222 us -> 136 us  [scatter(): lax.psum_scatter(a, ('q', 'm'), scatter_dimension=0, tiled=True)]
    all_gather x4 -> x0, blocking collectives: 84.6 us -> none  [the longest x1 26.1 us: on_device(): lax.all_gather(w_out.astype(jnp.bfloat16), 'dp', axis=1, tiled=True)]
    unnamed x17 -> x5, waiting for transfers between devices: 161 us -> 79.8 us
    convert_element_type x22 -> x9, other arithmetic: 86.7 us -> 13 us  [the longest x1 4.65 us: on_device(): gtok = (d_one + core_sum(term.astype(bf))).astype(bf)]
    unnamed x2 -> x0, blocking collectives: 60.2 us -> none
  transfers between devices with their start and end apart: 14 -> 17, of which waited for: 11 -> 14; matrix products, arithmetic and copies ran while one was open for 6% -> 13% of each run, Pallas kernels for 0% -> 8%
where the time goes in v1:
time: 622 us; the launch traced here: 611 us
  waiting for transfers between devices  301 us (48%)
  matrix products  99.1 us (16%)
  Pallas kernels  91.5 us (15%)
  other arithmetic  41.6 us (7%)
  local copies, waits for them, and re-layouts  30.4 us (5%)
  starting transfers between devices  30.2 us (5%)
  between operations  16.4 us (3%)
    reduce_scatter x1, waiting for transfers between devices, scatter(): lax.psum_scatter(a, ('q', 'm'), scatter_dimension=0, tiled=True)  136 us
    unnamed x5, waiting for transfers between devices  79.8 us
    all_gather x2, waiting for transfers between devices, gather(): lax.all_gather(lax.ppermute(a, ('c', 'm'), DIAG), ('q', 'm'), axis=0, til...  54.5 us
    pallas_call x1, Pallas kernels, attn_fwd(): pl.pallas_call(functools.partial(fwd_kernel, n, cols), out_shape=(S((P, n...  50.6 us
    dot_general x8, matrix products, dot(): return jnp.dot(a, b, preferred_element_type=f32)  48.6 us
    pallas_call x1, Pallas kernels, attn_bwd(): pl.pallas_call(functools.partial(bwd_kernel, n, heads), out_shape=S((3, n...  40.9 us
    dot_general x8, matrix products, dot_nt(): return lax.dot_general(a, b, NT, preferred_element_type=f32)  38.4 us
    unnamed x45, local copies, waits for them, and re-layouts  19.8 us
  transfers between devices with their start and end apart: 17, of which 14 were waited for; matrix products, arithmetic and copies ran while one was open for 13% of the time, Pallas kernels for 8%

profile of v1, /device:TPU:1, one launch (start us, length us, event | category | flops | bytes accessed | tf_op | source)
XLA Modules:
  0.0 610.6 jit_solution(17192812772158413623)
XLA Ops:
  11.6 4.5 collective-permute-start.1
  22.8 3.6 collective-permute-start.4
  26.4 5.4 collective-permute-done.4
  33.2 3.8 collective-permute-done.2
  52.5 31.4 %all-gather.3.cloned.1.call-done = bf16[768,1664]{1,0:T(8,128)(2,1)} async-done(((bf16[48,1664]{1,0:T(8,128)(2,1)}), bf16[768,1664]{1,0:T(8,128)(2,1)}) %all-gather.3.cloned.1.call-update) | async-done | bytes 2555920 | tf_op jit(solution)/shard_map/all_gather | solution.py:193
  86.7 50.6 %attn_fwd.1 = (bf16[4,1536,128]{2,1,0:T(8,128)(2,1)}, bf16[4,1536,128]{2,1,0:T(8,128)(2,1)}, bf16[4,1536,128]{2,1,0:T(8,128)(2,1)}, f32[4,128,1536]{2,1,0:T(8,12...) custom-call(bf16[1536,768]{1,0:T(8,128)(2,1)} %broadcast_select_fusion.1.tok, bf16[768,1152]{1,0:T(8,128)(2,1)} %slice.106.w, ...), custom_call_target="tpu_custom_call" | custom-call | tf_op jit(solution)/shard_map/attn_fwd/pallas_call | solution.py:85
  139.2 3.4 convolution_convert_fusion.4
  153.0 23.1 %all-gather.5.cloned.1.call-done = bf16[768,3840]{1,0:T(8,128)(2,1)} async-done(((bf16[48,3840]{1,0:T(8,128)(2,1)}), bf16[768,3840]{1,0:T(8,128)(2,1)}) %all-gather.5.cloned.1.call-update) | async-done | bytes 5898256 | tf_op jit(solution)/shard_map/all_gather | solution.py:193
  176.1 8.7 %fusion.13 = f32[1536,1280]{1,0:T(8,128)} fusion(bf16[1536,768]{1,0:T(8,128)(2,1)} %multiply_convert_fusion.4, bf16[768,3840]{1,0:T(8,128)(2,1)} %all-gather.5.cloned.1.call-done), kind=kOutput, calls=%fused_computation.41 | convolution fusion | flops 3019898880 | bytes 12189696 | tf_op jit(solution)/shard_map/dot_general | solution.py:12
  184.8 7.9 %multiply_convert_fusion.2 = (bf16[1536,1280]{1,0:T(8,128)(2,1)S(1)}, f32[1536,1280]{1,0:T(8,128)}) fusion(f32[1536,1280]{1,0:T(8,128)} %fusion.13, bf16[1536,768]{1,0:T(8,128)(2,1)S(1)} %copy-done.5, bf16[768,3840]{1,0:T(8,128)(2,1)S(1)} %copy-done.9), kind=kOutput, calls=%fused_computation.2 | convolution fusion | flops 3031695360 | bytes 23986176 | tf_op jit(solution)/shard_map/dot_general | solution.py:12
  194.7 3.5 convolution_convert_fusion.3
  200.1 4.1 collective-permute-done.5
  212.6 12.0 %multiply_convert_fusion.1 = (bf16[1536,1280]{1,0:T(8,128)(2,1)}, bf16[1536,1280]{1,0:T(8,128)(2,1)S(1)}) fusion(f32[1536,1280]{1,0:T(8,128)} %fusion.13, f32[1536,1280]{1,0:T(8,128)} %get-tuple-element.95, bf16[768,3840]{1,0:T(8,128)(2,1)} %all-gather.5.cloned.1.call-done, f32[1536,768]{1,0:T(8,128)S(1)} %get-tuple-element.80), kind=kOutput, calls=%fused_computation.1 | convolution fusion | flops 3046637568 | bytes 30277632 | tf_op jit(solution)/shard_map/dot_general | solution.py:12
  224.6 6.3 %fusion.8 = f32[1536,768]{1,0:T(8,128)S(1)} fusion(bf16[1536,1280]{1,0:T(8,128)(2,1)S(1)} %get-tuple-element.79, bf16[768,3840]{1,0:T(8,128)(2,1)} %all-gather.5.cloned.1.call-done), kind=kOutput, calls=%fused_computation.36 | convolution fusion | flops 3019898880 | bytes 10616832 | tf_op jit(solution)/shard_map/dot_general | solution.py:13
  230.9 5.1 add_convert_fusion.2
  236.4 4.2 collective-permute-done.8
  249.4 40.9 %attn_bwd.1 = bf16[3,1536,512]{2,1,0:T(8,128)(2,1)} custom-call(bf16[4,1536,128]{2,1,0:T(8,128)(2,1)} %get-tuple-element.18.q_s, bf16[4,1536,128]{2,1,0:T(8,128)(2,1)} %get-tuple-element.19.k_s, bf16[4,1536,128]{2,1,0:T(8,128)(2,1)} %get-tuple-element.20.v_s, f32[4,128,1536]{2,1,0:T(8,128)} %get-tuple-element.21.m_t, ...), custom_call_target="tpu_custom_call" | custom-call | tf_op jit(solution)/shard_map/attn_bwd/pallas_call | solution.py:147
  290.3 4.0 fusion.20
  294.3 4.0 fusion.19
  298.3 4.0 fusion.18
  302.3 5.4 fusion.17
  308.5 4.6 copy.56
  313.6 5.5 convolution_convert_fusion.1
  328.9 5.8 fusion.16
  334.7 5.9 fusion.15
  340.6 6.5 %add_convert_fusion.1 = bf16[1536,768]{1,0:T(8,128)(2,1)S(1)} fusion(f32[1536,768]{1,0:T(8,128)} %fusion.15, f32[1536,768]{1,0:T(8,128)} %fusion.16, bf16[3,1536,512]{2,1,0:T(8,128)(2,1)} %attn_bwd.1, bf16[768,1664]{1,0:T(8,128)(2,1)} %all-gather.3.cloned.1.call-done, s32[512]{0:T(512)S(1)} %iota_shift-right-logical_fusion, s32[512]{0:T(512)S(1)} %broadcast_add_fusion, ...), kind=kOutput, calls=%fused_computation.14 | convolution fusion | flops 1515847680 | bytes 13963776 | tf_op jit(solution)/shard_map/dot_general | solution.py:13
  351.8 4.6 add_convert_fusion
  356.4 3.4 collective-permute-start.10
  359.8 79.8 %reduce-scatter.7.cloned.1.call-done = bf16[48,1664]{1,0:T(8,128)(2,1)} async-done(((bf16[768,1664]{1,0:T(8,128)(2,1)}), bf16[48,1664]{1,0:T(8,128)(2,1)}) %reduce-scatter.7.cloned.1.call-update) | async-done | bytes 159760
  440.7 5.2 collective-permute-start.11
  452.6 135.6 %reduce-scatter.5.cloned.1.call-done = bf16[48,3840]{1,0:T(8,128)(2,1)} async-done(((bf16[768,3840]{1,0:T(8,128)(2,1)}), bf16[48,3840]{1,0:T(8,128)(2,1)}) %reduce-scatter.5.cloned.1.call-update) | async-done | bytes 368656 | tf_op jit(solution)/shard_map/reduce_scatter | solution.py:241
  588.2 5.5 collective-permute-start.12
  (125 shorter events, 96.0 us)
Async XLA Ops:
  7.2 76.7 %all-gather.3.cloned.1.call-start = ((), (), s32[]{:S(2)}) async-start(), calls=%async_computation.2 | async-start | bytes 2715648 | tf_op jit(solution)/shard_map/all_gather | solution.py:193
  11.6 7.5 %collective-permute-start.1 = (bf16[48,1664]{1,0:T(8,128)(2,1)S(1)}, bf16[48,1664]{1,0:T(8,128)(2,1)S(1)}, u32[]{:S(2)}, u32[]{:S(2)}) collective-permute-start(bf16[48,1664]{1,0:T(8,128)(2,1)S(1)} %constant_dynamic-update-slice_fusion), channel_id=1, source_target_pairs={{0,0},{3,3},{1,2},{2,1},{4,4},{7,7},{5,6},{6,5},{8,8},{11,11},{9,1... | collective-permute-start | bytes 479240 | tf_op jit(solution)/shard_map/ppermute | solution.py:193
  19.8 156.3 %all-gather.5.cloned.1.call-start = ((), (), s32[]{:S(2)}) async-start(), calls=%async_computation.3 | async-start | bytes 6266880 | tf_op jit(solution)/shard_map/all_gather | solution.py:193
  22.8 9.0 %collective-permute-start.4 = (bf16[48,3840]{1,0:T(8,128)(2,1)S(1)}, bf16[48,3840]{1,0:T(8,128)(2,1)S(1)}, u32[]{:S(2)}, u32[]{:S(2)}) collective-permute-start(bf16[48,3840]{1,0:T(8,128)(2,1)S(1)} %pad_maximum_fusion.1), channel_id=1, source_target_pairs={{0,0},{3,3},{1,2},{2,1},{4,4},{7,7},{5,6},{6,5},{8,8},{11,11},{9,1... | collective-permute-start | bytes 1105928 | tf_op jit(solution)/shard_map/ppermute | solution.py:193
  32.6 407.0 %reduce-scatter.7.cloned.1.call-start = ((), (), s32[]{:S(2)}) async-start(), calls=%async_computation.5 | async-start | bytes 2715648
  32.6 16.6 %collective-permute-start = (bf16[1536,768]{1,0:T(8,128)(2,1)}, bf16[1536,768]{1,0:T(8,128)(2,1)}, u32[]{:S(2)}, u32[]{:S(2)}) collective-permute-start(bf16[1536,768]{1,0:T(8,128)(2,1)} %param.12), channel_id=1, source_target_pairs={{0,2},{2,0},{1,3},{3,1},{4,6},{6,4},{5,7},{7,5},{8,10},{10,8},{9,1... | collective-permute-start | bytes 7077896 | tf_op jit(solution)/shard_map/ppermute | solution.py:186
  32.7 4.3 collective-permute-start.2
  139.2 8.6 %copy-start.2 = (bf16[1536,768]{1,0:T(8,128)(2,1)S(1)}, bf16[1536,768]{1,0:T(8,128)(2,1)}, u32[]{:S(2)}) copy-start(bf16[1536,768]{1,0:T(8,128)(2,1)} %broadcast_select_fusion.1.tok) | copy-start | bytes 7077892
  142.6 5.1 collective-permute-start.3
  148.9 2.2 copy-start
  176.1 8.7 %copy-start.5 = (bf16[1536,768]{1,0:T(8,128)(2,1)S(1)}, bf16[1536,768]{1,0:T(8,128)(2,1)}, u32[]{:S(2)}) copy-start(bf16[1536,768]{1,0:T(8,128)(2,1)} %multiply_convert_fusion.4) | copy-start | bytes 7077892
  176.1 8.7 %copy-start.9 = (bf16[768,3840]{1,0:T(8,128)(2,1)S(1)}, bf16[768,3840]{1,0:T(8,128)(2,1)}, u32[]{:S(2)}) copy-start(bf16[768,3840]{1,0:T(8,128)(2,1)} %all-gather.5.cloned.1.call-done) | copy-start | bytes 17694724
  176.1 28.1 %slice-start = ((s8[4718592]{0:T(1024)(128)(4,1)}), s8[4194304]{0:T(1024)(128)(4,1)S(1)}, s32[]{:S(2)}) async-start(s8[4718592]{0:T(1024)(128)(4,1)} %bitcast.55), calls=%async_computation.6 | async-start | bytes 8388608
  184.8 19.4 %slice-start.1 = ((s8[4718592]{0:T(1024)(128)(4,1)}), s8[524288]{0:T(1024)(128)(4,1)S(1)}, s32[]{:S(2)}) async-start(s8[4718592]{0:T(1024)(128)(4,1)} %bitcast.55), calls=%async_computation.7 | async-start | bytes 1048576
  194.7 5.3 copy-start.4
  198.2 6.0 collective-permute-start.5
  200.0 7.5 %collective-permute-start.7 = (bf16[1536,768]{1,0:T(8,128)(2,1)S(1)}, bf16[1536,768]{1,0:T(8,128)(2,1)S(1)}, u32[]{:S(2)}, u32[]{:S(2)}) collective-permute-start(bf16[1536,768]{1,0:T(8,128)(2,1)S(1)} %copy-done.4), channel_id=1, source_target_pairs={{0,2},{2,0},{1,3},{3,1},{4,6},{6,4},{5,7},{7,5},{8,10},{10,8},{9,1... | collective-permute-start | bytes 7077896 | tf_op jit(solution)/shard_map/ppermute | solution.py:186
  212.6 30.3 %copy-start.1 = (f32[1536,768]{1,0:T(8,128)}, f32[1536,768]{1,0:T(8,128)S(1)}, u32[]{:S(2)}) copy-start(f32[1536,768]{1,0:T(8,128)S(1)} %get-tuple-element.80) | copy-start | bytes 14155780
  224.6 6.3 %copy-start.14 = (bf16[1536,1280]{1,0:T(8,128)(2,1)}, bf16[1536,1280]{1,0:T(8,128)(2,1)S(1)}, u32[]{:S(2)}) copy-start(bf16[1536,1280]{1,0:T(8,128)(2,1)S(1)} %get-tuple-element.79) | copy-start | bytes 11796484
  224.6 6.3 %copy-start.12 = (bf16[1536,1280]{1,0:T(8,128)(2,1)S(1)}, bf16[1536,1280]{1,0:T(8,128)(2,1)}, u32[]{:S(2)}) copy-start(bf16[1536,1280]{1,0:T(8,128)(2,1)} %get-tuple-element.78) | copy-start | bytes 11796484
  236.0 4.6 collective-permute-start.8
  307.8 5.8 copy-start.6
  313.1 275.1 %reduce-scatter.5.cloned.1.call-start = ((), (), s32[]{:S(2)}) async-start(), calls=%async_computation.4 | async-start | bytes 6266880 | tf_op jit(solution)/shard_map/reduce_scatter | solution.py:241
  313.6 5.6 copy-start.13
  313.6 8.9 %slice-start.2 = ((s8[4718592]{0:T(1024)(128)(4,1)}), s8[4194304]{0:T(1024)(128)(4,1)S(1)}, s32[]{:S(2)}) async-start(s8[4718592]{0:T(1024)(128)(4,1)} %bitcast.57), calls=%async_computation.8 | async-start | bytes 8388608
  319.2 3.4 slice-start.3
  319.2 3.4 copy-start.11
  347.1 4.6 collective-permute-start.9
  347.6 98.4 %collective-permute-start.6 = (bf16[1536,768]{1,0:T(8,128)(2,1)}, bf16[1536,768]{1,0:T(8,128)(2,1)}, u32[]{:S(2)}, u32[]{:S(2)}) collective-permute-start(bf16[1536,768]{1,0:T(8,128)(2,1)} %get-tuple-element.81), channel_id=1, source_target_pairs={{0,0},{3,3},{1,2},{2,1},{4,4},{7,7},{5,6},{6,5},{8,8},{11,11},{9,1... | collective-permute-start | bytes 7077896 | tf_op jit(solution)/shard_map/ppermute | solution.py:243
  356.4 89.6 %collective-permute-start.10 = (bf16[1536,768]{1,0:T(8,128)(2,1)}, bf16[1536,768]{1,0:T(8,128)(2,1)S(1)}, u32[]{:S(2)}, u32[]{:S(2)}) collective-permute-start(bf16[1536,768]{1,0:T(8,128)(2,1)} %add_convert_fusion), channel_id=1, source_target_pairs={{0,0},{3,3},{1,2},{2,1},{4,4},{7,7},{5,6},{6,5},{8,8},{11,11},{9,1... | collective-permute-start | bytes 7077896 | tf_op jit(solution)/shard_map/ppermute | solution.py:244
  440.7 11.0 %collective-permute-start.11 = (bf16[48,1664]{0,1:T(8,128)(2,1)S(1)}, bf16[48,1664]{0,1:T(8,128)(2,1)S(1)}, u32[]{:S(2)}, u32[]{:S(2)}) collective-permute-start(bf16[48,1664]{0,1:T(8,128)(2,1)S(1)} %copy.57), channel_id=1, source_target_pairs={{0,0},{3,3},{1,2},{2,1},{4,4},{7,7},{5,6},{6,5},{8,8},{11,11},{9,1... | collective-permute-start | bytes 479240 | tf_op jit(solution)/shard_map/ppermute | solution.py:241
  588.2 10.9 %collective-permute-start.12 = (bf16[48,3840]{1,0:T(8,128)(2,1)}, bf16[48,3840]{1,0:T(8,128)(2,1)S(1)}, u32[]{:S(2)}, u32[]{:S(2)}) collective-permute-start(bf16[48,3840]{1,0:T(8,128)(2,1)} %reduce-scatter.5.cloned.1.call-done), channel_id=1, source_target_pairs={{0,0},{3,3},{1,2},{2,1},{4,4},{7,7},{5,6},{6,5},{8,8},{11,11},{9,1... | collective-permute-start | bytes 1105928 | tf_op jit(solution)/shard_map/ppermute | solution.py:241
  (4 other events, 5.6 us)
Sparse Core Ops, SparseCore 0:
  19.9 63.9 all-gather.2
  86.7 89.3 all-gather.4
  313.2 126.2 reduce-scatter.6
  445.6 142.5 reduce-scatter.4
